TPU v7x, 256 devices: a whole 4x4x8 slice. The times are simulated.
256 devices in a mesh: section: 8 (over z_lo, x), row: 32 (over z_hi, y, core).
Axes of the slice: x: 4, y: 4, z: 8 (z_hi: 4, z_lo: 2; z = z_hi * 2 + z_lo), core: 2. Of those that a mesh axis runs over, the one named last changes fastest.
Arguments:
- sections: float32 [8, 4096, 4096], P('section', None, 'row'), may hold values from -18 to 18
- preceding: float32 [4096, 4096], P(None, 'row'), may hold values from -18 to 18
Outputs:
- surface: float32 [8, 4096, 4096], P('section', None, 'row')
- peaks: float32 [8], P('section')
All inputs are finite; a program needn't handle non-finite values.
Results may differ from a plain program's by a relative error of at most 0.0003.
Values sent between devices are 32-bit elements; how exact they have to be, the bound alone decides.
A program may use at most 128 MiB of HBM per device.

v0:
```python
import math

import jax
import jax.numpy as jnp
from jax import lax
from jax.sharding import PartitionSpec as P

NX = 4096
NY = 4096
RADIX = 32


floor_share = 0.02


def passed_along(value, axis, steps):
    count = lax.axis_size(axis)
    leading, last = (max(0, -steps), min(count, count - steps))
    return lax.ppermute(value, axis, [(source, source + steps) for source in range(leading, last)])


def phase_pair(rows, cols, modulus, sign):
    first = jnp.arange(rows, dtype=jnp.int32)[:, None]
    second = jnp.arange(cols, dtype=jnp.int32)[None, :]
    angle = sign * 2.0 * math.pi / modulus * (first * second % modulus).astype(jnp.float32)
    return (jnp.cos(angle), jnp.sin(angle))


def real_table(rows, cols, modulus, sign):
    cosine, sine = phase_pair(rows, cols, modulus, sign)
    return jnp.stack([cosine, sine], 0)


def complex_table(rows, cols, modulus, sign):
    cosine, sine = phase_pair(rows, cols, modulus, sign)
    return jnp.stack([jnp.stack([cosine, sine], 0), jnp.stack([-sine, cosine], 0)], 0)


def product(form, left, right):
    return jnp.einsum(
        form, left, right, precision=lax.Precision.HIGHEST, preferred_element_type=jnp.float32
    )


def twist(values, cosine, sine):
    real_part, imag_part = (values[0], values[1])
    return jnp.stack(
        [real_part * cosine - imag_part * sine, real_part * sine + imag_part * cosine], 0
    )


def forward_rows(pixels):
    count, width_x, local_y = pixels.shape
    outer = width_x // RADIX
    grid = pixels.reshape(count, RADIX, outer, local_y)
    values = product("snmy,cna->csamy", grid, real_table(RADIX, RADIX, RADIX, -1))
    turn_cos, turn_sin = phase_pair(RADIX, outer, width_x, -1)
    values = twist(values, turn_cos[None, :, :, None], turn_sin[None, :, :, None])
    values = product("csamy,cdmb->dsbay", values, complex_table(outer, outer, outer, -1))
    return values.reshape(2, count, width_x, local_y)


def forward_columns(values):
    count, local_x, whole_y = (values.shape[1], values.shape[2], values.shape[3])
    outer = whole_y // RADIX
    values = values.reshape(2, count, local_x, RADIX, outer)
    values = product("csxnm,cdna->dsxam", values, complex_table(RADIX, RADIX, RADIX, -1))
    turn_cos, turn_sin = phase_pair(RADIX, outer, whole_y, -1)
    values = twist(values, turn_cos, turn_sin)
    return product("csxam,cdmb->dsxab", values, complex_table(outer, outer, outer, -1))


def inverse_columns(values):
    count, local_x, radix_count, outer = (
        values.shape[1],
        values.shape[2],
        values.shape[3],
        values.shape[4],
    )
    whole_y = radix_count * outer
    values = product("csxab,cdbm->dsxam", values, complex_table(outer, outer, outer, 1))
    turn_cos, turn_sin = phase_pair(RADIX, outer, whole_y, 1)
    values = twist(values, turn_cos, turn_sin)
    values = product("csxam,cdan->dsxnm", values, complex_table(RADIX, RADIX, RADIX, 1))
    return values.reshape(2, count, local_x, whole_y)


def inverse_rows(values):
    count, width_x, local_y = (values.shape[1], values.shape[2], values.shape[3])
    outer = width_x // RADIX
    values = values.reshape(2, count, outer, RADIX, local_y)
    values = product("csbay,cdbm->dsamy", values, complex_table(outer, outer, outer, 1))
    turn_cos, turn_sin = phase_pair(RADIX, outer, width_x, 1)
    values = twist(values, turn_cos[None, :, :, None], turn_sin[None, :, :, None])
    cosine, sine = phase_pair(RADIX, RADIX, RADIX, 1)
    result = product("csamy,can->snmy", values, jnp.stack([cosine, -sine], 0))
    return result.reshape(count, width_x, local_y) / width_x


def spectra(pixels):
    values = forward_rows(pixels)
    values = lax.all_to_all(values, "row", split_axis=2, concat_axis=3, tiled=True)
    return forward_columns(values)


def cross_ratio(prior, own):
    prior_real, prior_imag = (prior[0], prior[1])
    own_real, own_imag = (own[0], own[1])
    cross_real = prior_real * own_real + prior_imag * own_imag
    cross_imag = prior_imag * own_real - prior_real * own_imag
    magnitude = jnp.sqrt(prior_real * prior_real + prior_imag * prior_imag) * jnp.sqrt(
        own_real * own_real + own_imag * own_imag
    )
    divisor = jnp.maximum(magnitude, floor_share * NX * NY)
    return jnp.stack([cross_real / divisor, cross_imag / divisor], 0)


def local(sections, preceding):
    first_device = lax.axis_index("section") == 0
    spectrum = spectra(jnp.concatenate([preceding[None], sections], 0))
    own = spectrum[:, 1:]
    moved = passed_along(own, "section", 1)
    leading = jnp.where(first_device, spectrum[:, :1], moved)
    prior = jnp.concatenate([leading, own[:, :-1]], 1)
    ratio = cross_ratio(prior, own)
    values = inverse_columns(ratio)
    values = lax.all_to_all(values, "row", split_axis=3, concat_axis=2, tiled=True)
    surface = inverse_rows(values)
    peaks = lax.pmax(jnp.max(surface, axis=(1, 2)), "row")
    return (surface, peaks)


def solution(mesh):
    in_specs = (P("section", None, "row"), P(None, "row"))
    out_specs = (P("section", None, "row"), P("section"))
    return jax.shard_map(local, mesh=mesh, in_specs=in_specs, out_specs=out_specs, check_vma=False)
```

profile of v0, /device:TPU:4, one launch (start us, length us, event | category | flops | bytes accessed | tf_op | source)
XLA Modules:
  0.0 630.8 jit_solution(8185405976995391736)
XLA Ops:
  1.4 2.8 copy.94
  4.2 2.5 copy.95
  6.9 8.3 %fusion.21 = f32[2,2,32,128,128]{4,2,3,1,0:T(8,128)S(1)} fusion(f32[1,32,128,128]{3,1,2,0:T(8,128)} %copy.95, f32[1,32,128,128]{3,1,2,0:T(8,128)S(1)} %copy.94, f32[1,32,32]{1,2,0:T(8,128)S(1)} %get-tuple-element.22, f32[1,32,32]{1,2,0:T(8,128)S(1)} %get-tuple-element.23), kind=kOutput, calls=%fused_computation.32 | convolution fusion | flops 806356992 | bytes 12591104 | tf_op jit(solution)/shard_map/snmy,cna->csamy/dot_general | solution.py:40
  18.1 24.1 %fusion.22 = f32[2,2,128,32,128]{4,2,3,1,0:T(8,128)S(1)} fusion(f32[2,2,32,128,128]{4,2,3,1,0:T(8,128)S(1)} %pad_maximum_fusion, f32[1,2,128,128]{2,3,0,1:T(8,128)S(1)} %get-tuple-element.15, f32[1,2,128,128]{2,3,0,1:T(8,128)S(1)} %get-tuple-element.14), kind=kOutput, calls=%fused_computation.33 | convolution fusion | flops 6442516480 | bytes 17039360 | tf_op jit(solution)/shard_map/csamy,cdmb->dsbay/dot_general | solution.py:40
  42.2 4.9 copy.99
  47.0 23.5 %copy.100 = f32[2,2,4096,128]{3,1,0,2:T(2,128)} copy(f32[2,2,4096,128]{3,2,1,0:T(8,128)S(1)} %bitcast.140) | data formatting | bytes 16777216 | tf_op jit(solution)/shard_map/reshape | solution.py:60
  70.5 11.6 %all-to-all-start = ((f32[2,2,4096,128]{3,1,0,2:T(2,128)}), f32[2,2,4096,128]{3,1,0,2:T(2,128)}, u32[]{:S(2)}, u32[]{:S(2)}) async-start(f32[2,2,4096,128]{3,1,0,2:T(2,128)} %copy.100), calls=%async_computation | async-start | bytes 16777216 | tf_op jit(solution)/shard_map/all_to_all | solution.py:102
  82.2 186.6 %all-to-all-done = f32[2,2,4096,128]{3,1,0,2:T(2,128)} async-done(((f32[2,2,4096,128]{3,1,0,2:T(2,128)}), f32[2,2,4096,128]{3,1,0,2:T(2,128)}, u32[]{:S(2)}, u32[]{:S(2)}) %all-to-all-start) | async-done | bytes 8388640 | tf_op jit(solution)/shard_map/all_to_all | solution.py:102
  268.8 16.2 %fusion.28 = f32[2,2,128,32,128]{4,3,2,1,0:T(8,128)S(1)} fusion(f32[2,2,32,128,128]{4,1,0,3,2:T(2,128)} %bitcast.28, f32[1,2,32,32]{2,3,1,0:T(8,128)S(1)} %get-tuple-element.19, f32[1,2,32,32]{2,3,1,0:T(8,128)S(1)} %get-tuple-element.18), kind=kOutput, calls=%fused_computation.35 | convolution fusion | flops 1610616832 | bytes 16793600 | tf_op jit(solution)/shard_map/csxnm,cdna->dsxam/dot_general | solution.py:40
  287.7 11.8 %fusion.25 = f32[2,2,128,32,128]{2,4,3,1,0:T(8,128)S(1)} fusion(f32[2,2,128,32,128]{4,3,2,1,0:T(8,128)S(1)} %pad_maximum_fusion.1, f32[1,2,128,128]{2,3,0,1:T(8,128)S(1)} %get-tuple-element.15, f32[1,2,128,128]{2,3,0,1:T(8,128)S(1)} %get-tuple-element.14), kind=kOutput, calls=%fused_computation.34 | convolution fusion | flops 6442516480 | bytes 17039360 | tf_op jit(solution)/shard_map/csxam,cdmb->dsxab/dot_general | solution.py:40
  299.5 2.4 slice.63
  304.0 3.1 collective-permute-start
  308.0 90.4 %collective-permute-done = f32[2,1,128,32,128]{2,4,3,1,0:T(8,128)} collective-permute-done((f32[2,1,128,32,128]{2,4,3,1,0:T(8,128)}, f32[2,1,128,32,128]{2,4,3,1,0:T(8,128)}, u32[]{:S(2)}, u32[]{:S(2)}) %collective-permute-start) | collective-permute-done | bytes 4194336 | tf_op jit(solution)/shard_map/ppermute | solution.py:19
  398.4 4.2 slice_select_fusion
  404.8 4.1 fusion.31
  412.6 5.5 copy.108
  418.1 7.9 %fusion.34 = f32[2,1,128,32,128]{4,3,2,0,1:T(8,128)} fusion(f32[2,128,32,128]{3,2,0,1:T(8,128)} %copy.108, f32[1,2,32,32]{2,3,1,0:T(8,128)S(1)} %get-tuple-element.17, f32[1,2,32,32]{2,3,1,0:T(8,128)S(1)} %get-tuple-element.16), kind=kOutput, calls=%fused_computation.37 | convolution fusion | flops 805310464 | bytes 8404992 | tf_op jit(solution)/shard_map/csxam,cdan->dsxnm/dot_general | solution.py:40
  425.9 5.3 copy.142
  431.2 101.1 %all_to_all.30 = f32[2,1,128,4096]{2,0,1,3:T(2,128)S(1)} all-to-all(f32[2,1,128,4096]{2,0,1,3:T(2,128)} %bitcast.142), channel_id=1, replica_groups=mesh['section'=8,'row'=32] {'row'}, dimensions={3} | all-to-all | bytes 8388608 | tf_op jit(solution)/shard_map/all_to_all | solution.py:127
  534.6 5.7 copy.111
  540.3 7.2 %fusion.37 = f32[2,1,32,128,128]{4,3,2,0,1:T(8,128)S(1)} fusion(f32[2,128,32,128]{3,2,1,0:T(8,128)} %bitcast.141, f32[1,2,128,128]{2,3,1,0:T(8,128)S(1)} %get-tuple-element.13, f32[1,2,128,128]{2,3,1,0:T(8,128)S(1)} %get-tuple-element.12), kind=kOutput, calls=%fused_computation.38 | convolution fusion | flops 3221291008 | bytes 8650752 | tf_op jit(solution)/shard_map/csbay,cdbm->dsamy/dot_general | solution.py:40
  549.4 5.3 fusion.76
  554.7 2.5 copy.115
  557.3 73.2 %pmax.7 = f32[1]{0:T(128)} all-reduce(f32[1]{0:T(128)} %bitcast.67), channel_id=1, replica_groups=mesh['section'=8,'row'=32] {'row'}, use_global_device_ids=true, to_apply=%region_1.2 | all-reduce | flops 1 | bytes 8 | tf_op jit(solution)/shard_map/pmax | solution.py:129
  (32 shorter events, 19.3 us)
Async XLA Ops:
  0.6 3.5 copy-start.2
  70.5 198.3 %all-to-all-start = ((f32[2,2,4096,128]{3,1,0,2:T(2,128)}), f32[2,2,4096,128]{3,1,0,2:T(2,128)}, u32[]{:S(2)}, u32[]{:S(2)}) async-start(f32[2,2,4096,128]{3,1,0,2:T(2,128)} %copy.100), calls=%async_computation | async-start | bytes 16777216 | tf_op jit(solution)/shard_map/all_to_all | solution.py:102
  299.5 4.5 copy-start
  304.0 94.4 %collective-permute-start = (f32[2,1,128,32,128]{2,4,3,1,0:T(8,128)}, f32[2,1,128,32,128]{2,4,3,1,0:T(8,128)}, u32[]{:S(2)}, u32[]{:S(2)}) collective-permute-start(f32[2,1,128,32,128]{2,4,3,1,0:T(8,128)} %slice.63), channel_id=1, source_target_pairs={{0,32},{32,64},{64,96},{96,128},{128,160},{160,192},{192,224},{1,3... | collective-permute-start | bytes 12582920 | tf_op jit(solution)/shard_map/ppermute | solution.py:19
  308.0 94.7 %copy-start.1 = (f32[2,2,128,32,128]{2,4,3,1,0:T(8,128)S(1)}, f32[2,2,128,32,128]{2,4,3,1,0:T(8,128)}, u32[]{:S(2)}) copy-start(f32[2,2,128,32,128]{2,4,3,1,0:T(8,128)} %copy-done) | copy-start | bytes 25165828
where the time goes:
time: 639 us; the launch traced here: 631 us
  waiting for transfers between devices  277 us (43%)
  blocking collectives  174 us (27%)
  matrix products  84.9 us (13%)
  local copies, waits for them, and re-layouts  59.6 us (9%)
  other arithmetic  19 us (3%)
  starting transfers between devices  14.7 us (2%)
    all_to_all x1, waiting for transfers between devices, spectra(): lax.all_to_all(values, 'row', split_axis=2, concat_axis=3, tiled=True)  187 us
    all_to_all x1, blocking collectives, local(): lax.all_to_all(values, 'row', split_axis=3, concat_axis=2, tiled=True)  101 us
    ppermute x1, waiting for transfers between devices, passed_along(): lax.ppermute(value, axis, [(source, source + steps) for source in range(l...  90.4 us
    dot_general x8, matrix products, product(): jnp.einsum(form, left, right, precision=lax.Precision.HIGHEST, preferred_...  84.9 us
    pmax x1, blocking collectives, local(): peaks = lax.pmax(jnp.max(surface, axis=(1, 2)), 'row')  73.2 us
    reshape x1, local copies, waits for them, and re-layouts, forward_rows(): return values.reshape(2, count, width_x, local_y)  23.5 us
  transfers between devices with their start and end apart: 2, of which 2 were waited for; matrix products, arithmetic and copies ran while one was open for 0% of the time, Pallas kernels for 0%

commit v1 on v0

v1 whole, which is shorter than its diff:
```python
import functools
import math

import jax
import jax.numpy as jnp
import ml_dtypes
import numpy as np
from jax import lax
from jax.experimental import pallas as pl
from jax.experimental.pallas import tpu as pltpu
from jax.sharding import PartitionSpec as P

MESH = pl.DeviceIdType.MESH
F32 = jnp.float32
BF16 = jnp.bfloat16

N = 4096
R = 32
L = 128
SEC = 8
ROW = 32
DEV = SEC * ROW
UNITS = 16
FLOOR = 0.02 * 4096 * 4096
VMEM_LIMIT = 48 << 20


def split(table):
    high = table.astype(ml_dtypes.bfloat16)
    low = (table - high.astype(np.float64)).astype(ml_dtypes.bfloat16)
    return np.stack([high, low], -3)


@functools.lru_cache(None)
def tables():
    n2 = np.arange(L)
    row = np.arange(L)
    fwd = np.zeros((UNITS, 16, 2, 8, 2, L))
    inv = np.zeros((UNITS, 2, L, 16, 2, 8))

    def angles(kx):
        turn = 2 * np.pi / N * (np.outer(kx, n2) % N)
        return np.cos(turn).reshape(-1, 8, L), np.sin(turn).reshape(-1, 8, L)

    for u in range(1, UNITS):
        c, s = angles(u + R * row)
        fwd[u, :, 0, :, 0], fwd[u, :, 0, :, 1] = c, s
        fwd[u, :, 1, :, 0], fwd[u, :, 1, :, 1] = -s, c
        ct, st = np.moveaxis(c, 2, 0), np.moveaxis(s, 2, 0)
        inv[u, 0, :, :, 0], inv[u, 0, :, :, 1] = ct, -st
        inv[u, 1, :, :, 0], inv[u, 1, :, :, 1] = st, ct
    for half, base in ((0, 0), (1, 16)):
        c, s = angles(base + R * np.arange(L // 2))
        js = slice(8 * half, 8 * half + 8)
        ti, tr = -s, c
        bi, br = -2 * s, 2 * c
        if half == 0:
            ti[0, 0] = (-1.0) ** n2
            bi[0, 0] = (-1.0) ** n2
            br[0, 0] = 1.0
        fwd[0, js, 0, :, half], fwd[0, js, 1, :, half] = tr, ti
        inv[0, half, :, js, 0] = np.moveaxis(br, 2, 0)
        inv[0, half, :, js, 1] = np.moveaxis(bi, 2, 0)
    fwd = split(fwd.reshape(UNITS, 2 * L, 2 * L))
    inv = split(inv.reshape(UNITS, 2 * L, 2 * L) / N)
    turn = 2 * np.pi / L * (np.outer(row, row) % L)
    c, s = np.cos(turn), np.sin(turn)
    lanes = split(np.block([[c, -s], [s, c]]))
    lanes_inv = split(np.block([[c, s], [-s, c]]))
    turn = 2 * np.pi / N * np.outer(np.arange(R + 1), row)
    twist = np.stack([np.cos(turn), np.sin(turn)], 1).astype(np.float32)
    twist = np.broadcast_to(twist[:, :, None, :], (R + 1, 2, 8, L)).copy()
    return fwd, inv, lanes, lanes_inv, twist


def turned(z, k, n, sign):
    k %= n
    re, im = z
    if k == 0:
        return z
    if 4 * k == n:
        return (-im, re) if sign > 0 else (im, -re)
    if 2 * k == n:
        return (-re, -im)
    if 8 * k == n:
        h = math.sqrt(0.5)
        return ((re - im) * h, (re + im) * h) if sign > 0 else ((re + im) * h, (im - re) * h)
    c, s = math.cos(2 * math.pi * k / n), sign * math.sin(2 * math.pi * k / n)
    return (re * c - im * s, re * s + im * c)


def add(a, b):
    return (a[0] + b[0], a[1] + b[1])


def sub(a, b):
    return (a[0] - b[0], a[1] - b[1])


def complex_dft(z, sign):
    n = len(z)
    if n == 1:
        return z
    even, odd = complex_dft(z[0::2], sign), complex_dft(z[1::2], sign)
    out = [None] * n
    for k in range(n // 2):
        t = turned(odd[k], k, n, sign)
        out[k], out[k + n // 2] = add(even[k], t), sub(even[k], t)
    return out


def real_dft(x):
    n = len(x)
    if n == 2:
        return [(x[0] + x[1], None), (x[0] - x[1], None)]
    even, odd = real_dft(x[0::2]), real_dft(x[1::2])
    out = [None] * (n // 2 + 1)
    out[0] = (even[0][0] + odd[0][0], None)
    out[n // 2] = (even[0][0] - odd[0][0], None)
    for k in range(1, n // 4):
        t = turned(odd[k], k, n, -1)
        out[k] = add(even[k], t)
        d = sub(even[k], t)
        out[n // 2 - k] = (d[0], -d[1])
    out[n // 4] = (even[n // 4][0], -odd[n // 4][0])
    return out


def real_dft_back(z):
    n = 2 * (len(z) - 1)
    if n == 2:
        return [z[0][0] + z[1][0], z[0][0] - z[1][0]]
    even, odd = [None] * (n // 4 + 1), [None] * (n // 4 + 1)
    even[0] = (z[0][0] + z[n // 2][0], None)
    odd[0] = (z[0][0] - z[n // 2][0], None)
    for k in range(1, n // 4):
        mirror = (z[n // 2 - k][0], -z[n // 2 - k][1])
        even[k] = add(z[k], mirror)
        odd[k] = turned(sub(z[k], mirror), k, n, 1)
    even[n // 4] = (z[n // 4][0] * 2.0, None)
    odd[n // 4] = (z[n // 4][1] * -2.0, None)
    out = [None] * n
    out[0::2], out[1::2] = real_dft_back(even), real_dft_back(odd)
    return out


def parts(value):
    high = value.astype(BF16)
    return high, (value - high.astype(F32)).astype(BF16)


def dot(a, b):
    return jnp.dot(a, b, preferred_element_type=F32)


def table_times(table_ref, value):
    high, low = parts(value)
    both = dot(table_ref[0], jnp.concatenate([high, low], 1))
    width = value.shape[1]
    return both[:, :width] + both[:, width:] + dot(table_ref[1], high)


def times_table(value, table_ref):
    high, low = parts(value)
    return dot(high, table_ref[0]) + dot(low, table_ref[0]) + dot(high, table_ref[1])


def x_first(pixels_ref, a_ref):
    @pl.loop(0, L // 8)
    def _(g):
        rows = pl.ds(pl.multiple_of(g * 8, 8), 8)
        more = pl.ds(pl.multiple_of(g * 8 + L, 8), 8)
        out = real_dft([pixels_ref[n, rows, :] for n in range(R)])
        a_ref[0, rows, :] = out[0][0]
        a_ref[0, more, :] = out[R // 2][0]
        for u in range(1, UNITS):
            a_ref[u, rows, :] = out[u][0]
            a_ref[u, more, :] = out[u][1]


def x_unit(table_ref, value):
    return table_times(table_ref, value).reshape(16, 2, 8, L)


def x_last(b_ref, out_ref):
    def body(g, top):
        rows = pl.ds(pl.multiple_of(g * 8, 8), 8)
        more = pl.ds(pl.multiple_of(g * 8 + L, 8), 8)
        z = [(b_ref[0, rows, :], None)]
        z += [(b_ref[u, rows, :], b_ref[u, more, :]) for u in range(1, UNITS)]
        z += [(b_ref[0, more, :], None)]
        out = real_dft_back(z)
        for n in range(R):
            out_ref[n, rows, :] = out[n]
        while len(out) > 1:
            out = [jnp.maximum(a, b) for a, b in zip(out[0::2], out[1::2])]
        return jnp.maximum(top, out[0])

    return lax.fori_loop(0, L // 8, body, jnp.full((8, L), -jnp.inf, F32))


def y_forward(tile_ref, twist_ref, lanes_ref, v_ref, own_ref, mirror_ref, special):
    z = complex_dft([(tile_ref[p, 0], tile_ref[p, 1]) for p in range(R)], -1)
    for a in range(R):
        re, im = z[a]
        if a:
            c, s = twist_ref[a, 0], twist_ref[a, 1]
            re, im = re * c + im * s, im * c - re * s
        v_ref[a, :, :L] = re
        v_ref[a, :, L:] = im
    own_ref[...] = times_table(v_ref[...].reshape(R * 8, 2 * L), lanes_ref).reshape(R, 8, 2 * L)

    @pl.when(special)
    def _():
        c, s = twist_ref[R, 0], twist_ref[R, 1]

        @pl.loop(0, R)
        def _(a):
            first = a == 0
            back = lax.rem(R - a, R)
            re, im = v_ref[back, :, :L], -v_ref[back, :, L:]
            mirror_ref[a, :, :L] = jnp.where(first, re, re * c + im * s)
            mirror_ref[a, :, L:] = jnp.where(first, im, im * c - re * s)

        value = mirror_ref[...].reshape(R * 8, 2 * L)
        mirror_ref[...] = times_table(value, lanes_ref).reshape(R, 8, 2 * L)


def phase(pr, pi, our, oi):
    re = pr * our + pi * oi
    im = pi * our - pr * oi
    scale = lax.rsqrt(jnp.maximum(re * re + im * im, FLOOR * FLOOR))
    return re * scale, im * scale


def y_ratio(prior_ref, own_ref, prior_mirror_ref, own_mirror_ref, v_ref, special):
    re, im = phase(prior_ref[:, :, :L], prior_ref[:, :, L:], own_ref[:, :, :L], own_ref[:, :, L:])
    v_ref[:, :, :L] = re
    v_ref[:, :, L:] = im

    @pl.when(special)
    def _():
        def both(ref, mirror, a):
            re, im, mre, mim = ref[a, :, :L], ref[a, :, L:], mirror[a, :, :L], mirror[a, :, L:]
            low = ((re + mre) * 0.5, (im + mim) * 0.5)
            high = ((im - mim) * 0.5, (mre - re) * 0.5)
            return low, high

        packed = lax.broadcasted_iota(jnp.int32, (8, L), 0) == 0

        @pl.loop(0, R)
        def _(a):
            prior_low, prior_high = both(prior_ref, prior_mirror_ref, a)
            own_low, own_high = both(own_ref, own_mirror_ref, a)
            low = phase(*prior_low, *own_low)
            high = phase(*prior_high, *own_high)
            v_ref[a, :, :L] = jnp.where(packed, low[0] - high[1], v_ref[a, :, :L])
            v_ref[a, :, L:] = jnp.where(packed, low[1] + high[0], v_ref[a, :, L:])


def y_back(v_ref, twist_ref, lanes_inv_ref, out_ref):
    v_ref[...] = times_table(v_ref[...].reshape(R * 8, 2 * L), lanes_inv_ref).reshape(R, 8, 2 * L)
    z = []
    for a in range(R):
        re, im = v_ref[a, :, :L], v_ref[a, :, L:]
        if a:
            c, s = twist_ref[a, 0], twist_ref[a, 1]
            re, im = re * c - im * s, im * c + re * s
        z.append((re, im))
    z = complex_dft(z, 1)
    for p in range(R):
        out_ref[p, 0] = z[p][0]
        out_ref[p, 1] = z[p][1]


def forward_kernel(sec_ref, pre_ref, fwd_ref, x_ref, xp_ref, a_ref):
    s = lax.axis_index("section")
    x_first(pre_ref, a_ref)
    for h in range(2):
        u = 2 * s + h
        xp_ref[pl.ds(h * 16, 16)] = x_unit(fwd_ref.at[u], a_ref[u])
    x_first(sec_ref, a_ref)

    @pl.loop(0, UNITS)
    def _(u):
        x_ref[pl.ds(u * 16, 16)] = x_unit(fwd_ref.at[u], a_ref[u])


def middle_kernel(r_ref, rp_ref, lanes_ref, lanes_inv_ref, twist_ref, y_ref, v_ref, spec_ref, mirror_ref):
    special = (lax.axis_index("section") == 0) & (lax.axis_index("row") == 0)
    y_forward(rp_ref, twist_ref, lanes_ref, v_ref, spec_ref.at[1], mirror_ref.at[1], special)

    @pl.loop(0, SEC)
    def _(s):
        own, prior = lax.rem(s, 2), lax.rem(s + 1, 2)
        y_forward(r_ref.at[s], twist_ref, lanes_ref, v_ref, spec_ref.at[own], mirror_ref.at[own], special)
        y_ratio(spec_ref.at[prior], spec_ref.at[own], mirror_ref.at[prior], mirror_ref.at[own], v_ref, special)
        y_back(v_ref, twist_ref, lanes_inv_ref, y_ref.at[s])


def back_kernel(q_ref, inv_ref, out_ref, top_ref, b_ref):
    @pl.loop(0, UNITS)
    def _(u):
        value = q_ref[pl.ds(u * 16, 16)].reshape(2 * L, L)
        b_ref[u] = table_times(inv_ref.at[u], value)

    top_ref[...] = x_last(b_ref, out_ref)


def here():
    return lax.axis_index("section"), lax.axis_index("row")


def exchange_kernel(with_first, *refs):
    if with_first:
        x_ref, xp_ref, o_ref, op_ref, send_sem, recv_sem, loc_sem = refs
    else:
        x_ref, o_ref, send_sem, recv_sem, loc_sem = refs
    s, p = here()
    bar = pltpu.get_barrier_semaphore()

    @pl.loop(1, DEV)
    def _(i):
        to = ((s + i // ROW) % SEC, (p + i % ROW) % ROW)
        pl.semaphore_signal(bar, inc=1, device_id=to, device_id_type=MESH)

    pl.semaphore_wait(bar, DEV - 1)
    me = s * ROW + p
    own = [pltpu.make_async_copy(x_ref.at[me], o_ref.at[me], loc_sem.at[0])]
    if with_first:
        own.append(pltpu.make_async_copy(xp_ref.at[p], op_ref.at[p], loc_sem.at[1]))
    for copy in own:
        copy.start()
    if with_first:

        @pl.loop(1, ROW)
        def _(i):
            to = (p + i) % ROW
            pltpu.make_async_remote_copy(
                xp_ref.at[to], op_ref.at[p], send_sem.at[1], recv_sem.at[1], device_id=(s, to), device_id_type=MESH
            ).start()

    @pl.loop(1, DEV)
    def _(i):
        ts, tp = (s + i // ROW) % SEC, (p + i % ROW) % ROW
        pltpu.make_async_remote_copy(
            x_ref.at[ts * ROW + tp], o_ref.at[me], send_sem.at[0], recv_sem.at[0], device_id=(ts, tp), device_id_type=MESH
        ).start()

    for copy in own:
        copy.wait()
    for sem in (recv_sem, send_sem):
        count = pl.ds(0, DEV - 1)
        pltpu.make_async_copy(x_ref.at[count], o_ref.at[count], sem.at[0]).wait()
        if with_first:
            count = pl.ds(0, ROW - 1)
            pltpu.make_async_copy(xp_ref.at[count], op_ref.at[count], sem.at[1]).wait()


def peak_kernel(top_ref, peak_ref, mine_ref, all_ref, send_sem, recv_sem):
    s, p = here()
    bar = pltpu.get_barrier_semaphore()

    @pl.loop(1, ROW)
    def _(i):
        pl.semaphore_signal(bar, inc=1, device_id=(s, (p + i) % ROW), device_id_type=MESH)

    pl.semaphore_wait(bar, ROW - 1)
    mine_ref[...] = top_ref[...]
    all_ref[p] = top_ref[...]

    @pl.loop(1, ROW)
    def _(i):
        pltpu.make_async_remote_copy(
            mine_ref, all_ref.at[p], send_sem, recv_sem, device_id=(s, (p + i) % ROW), device_id_type=MESH
        ).start()

    count = pl.ds(0, ROW - 1)
    for sem in (recv_sem, send_sem):
        pltpu.make_async_copy(all_ref.at[count], all_ref.at[count], sem).wait()
    peak_ref[...] = jnp.max(all_ref[...], axis=0)


VMEM = pl.BlockSpec(memory_space=pltpu.VMEM)
ANY = pl.BlockSpec(memory_space=pl.ANY)


def f32(*shape):
    return jax.ShapeDtypeStruct(shape, F32)


def call(kernel, args, outs, scratch, place=VMEM, collective=None):
    extra = {} if collective is None else dict(collective_id=collective, has_side_effects=True)
    return pl.pallas_call(
        kernel,
        out_shape=outs,
        in_specs=[place] * len(args),
        out_specs=jax.tree.map(lambda _: place, outs),
        scratch_shapes=scratch,
        compiler_params=pltpu.CompilerParams(vmem_limit_bytes=VMEM_LIMIT, **extra),
    )(*args)


def local(sections, preceding):
    fwd, inv, lanes, lanes_inv, twist = (jnp.asarray(t) for t in tables())
    block = (2, 8, L)
    sem = pltpu.SemaphoreType.DMA
    x, xp = call(
        forward_kernel,
        (sections.reshape(R, L, L), preceding.reshape(R, L, L), fwd),
        (f32(DEV, *block), f32(ROW, *block)),
        [pltpu.VMEM((UNITS, 2 * L, L), F32)],
    )
    r, rp = call(
        functools.partial(exchange_kernel, True), (x, xp), (f32(DEV, *block), f32(ROW, *block)), [sem((2,))] * 3, ANY, 1
    )
    y = call(
        middle_kernel,
        (r.reshape(SEC, ROW, *block), rp, lanes, lanes_inv, twist),
        f32(SEC, ROW, *block),
        [pltpu.VMEM((R, 8, 2 * L), F32)] + [pltpu.VMEM((2, R, 8, 2 * L), F32)] * 2,
    )
    q = call(functools.partial(exchange_kernel, False), (y.reshape(DEV, *block),), f32(DEV, *block), [sem((2,))] * 3, ANY, 2)
    surface, top = call(
        back_kernel, (q, inv), (f32(R, L, L), f32(8, L)), [pltpu.VMEM((UNITS, 2 * L, L), F32)]
    )
    peak = call(
        peak_kernel, (top,), f32(8, L), [pltpu.VMEM((8, L), F32), pltpu.VMEM((ROW, 8, L), F32), sem, sem], VMEM, 3
    )
    return surface.reshape(1, N, L), jnp.max(peak).reshape(1)


def solution(mesh):
    in_specs = (P("section", None, "row"), P(None, "row"))
    out_specs = (P("section", None, "row"), P("section"))
    return jax.shard_map(local, mesh=mesh, in_specs=in_specs, out_specs=out_specs, check_vma=False)
```

time: 639 us -> 172 us (0.27)
  the two profiles are of different devices: /device:TPU:4 before, /device:TPU:1 now
where the time goes in v1:
time: 172 us
  Pallas kernels  169 us (98%)
    pallas_call x6, Pallas kernels, call(): pl.pallas_call(kernel, out_shape=outs, in_specs=[place] * len(args), out_...  169 us

profile of v1, /device:TPU:1, one launch (start us, length us, event | category | flops | bytes accessed | tf_op | source)
XLA Modules:
  0.0 171.8 jit_solution(1629664826360036423)
XLA Ops:
  0.6 0.0 copy-start
  0.6 1.6 copy-done
  2.2 8.4 %shard_map.86 = (f32[256,2,8,128]{3,2,1,0:T(8,128)S(1)}, f32[32,2,8,128]{3,2,1,0:T(8,128)S(1)}) custom-call(f32[32,128,128]{2,1,0:T(8,128)S(1)} %bitcast.8, f32[32,128,128]{2,1,0:T(8,128)} %bitcast.9, bf16[16,2,256,256]{3,2,1,0:T(8,128)(2,1)} %constant.12.clone.fwd_ref), custom_call_target="tpu_custom_call" | custom-call | tf_op jit(solution)/shard_map/pallas_call | solution.py:394
  10.6 0.0 copy-start.1
  10.6 0.0 copy-start.2
  10.6 0.0 copy-start.3
  10.6 69.5 %shard_map.87 = (f32[256,2,8,128]{3,2,1,0:T(8,128)S(1)}, f32[32,2,8,128]{3,2,1,0:T(8,128)S(1)}) custom-call(f32[256,2,8,128]{3,2,1,0:T(8,128)S(1)} %get-tuple-element.8.refs_0_, f32[32,2,8,128]{3,2,1,0:T(8,128)S(1)} %get-tuple-element.9.refs_1_), custom_call_target="tpu_custom_call" | custom-call | tf_op jit(solution)/shard_map/pallas_call | solution.py:394
  80.1 0.0 copy-done.1
  80.1 0.0 copy-done.2
  80.1 0.0 copy-done.3
  80.1 5.9 %shard_map.88 = f32[8,32,2,8,128]{4,3,2,1,0:T(8,128)S(1)} custom-call(f32[8,32,2,8,128]{4,3,2,1,0:T(8,128)S(1)} %bitcast.7, f32[32,2,8,128]{3,2,1,0:T(8,128)S(1)} %get-tuple-element.11.rp_ref, bf16[2,256,256]{2,1,0:T(8,128)(2,1)S(1)} %copy-done.3, bf16[2,256,256]{2,1,0:T(8,128)(2,1)S(1)} %copy-done.2, f32[33,2,8,128]{3,2,1,0:T(8,128)S(1)} %copy-done.1), custom_call_target="tpu_custom_call" | custom-call | tf_op jit(solution)/shard_map/pallas_call | solution.py:394
  86.0 64.3 %shard_map.89.q_ref = f32[256,2,8,128]{3,2,1,0:T(8,128)S(1)} custom-call(f32[256,2,8,128]{3,2,1,0:T(8,128)S(1)} %bitcast.6), custom_call_target="tpu_custom_call" | custom-call | tf_op jit(solution)/shard_map/pallas_call | solution.py:394
  150.4 8.1 %shard_map.90 = (f32[32,128,128]{2,1,0:T(8,128)}, f32[8,128]{1,0:T(8,128)S(1)}) custom-call(f32[256,2,8,128]{3,2,1,0:T(8,128)S(1)} %shard_map.89.q_ref, bf16[16,2,256,256]{3,2,1,0:T(8,128)(2,1)} %constant.13.clone.inv_ref), custom_call_target="tpu_custom_call" | custom-call | tf_op jit(solution)/shard_map/pallas_call | solution.py:394
  158.5 12.7 %shard_map.91 = f32[8,128]{1,0:T(8,128)S(1)} custom-call(f32[8,128]{1,0:T(8,128)S(1)} %get-tuple-element.13.top_ref), custom_call_target="tpu_custom_call" | custom-call | tf_op jit(solution)/shard_map/pallas_call | solution.py:394
  171.2 0.6 reduce_max.9
Async XLA Ops:
  0.6 1.6 copy-start
  10.6 69.5 %copy-start.1 = (f32[33,2,8,128]{3,2,1,0:T(8,128)S(1)}, f32[33,2,8,128]{3,2,1,0:T(8,128)}, u32[]{:S(2)}) copy-start(f32[33,2,8,128]{3,2,1,0:T(8,128)} %constant.16.clone.twist_ref) | copy-start | bytes 811012
  10.6 69.5 %copy-start.2 = (bf16[2,256,256]{2,1,0:T(8,128)(2,1)S(1)}, bf16[2,256,256]{2,1,0:T(8,128)(2,1)}, u32[]{:S(2)}) copy-start(bf16[2,256,256]{2,1,0:T(8,128)(2,1)} %constant.15.clone.lanes_inv_ref) | copy-start | bytes 786436
  10.6 69.5 %copy-start.3 = (bf16[2,256,256]{2,1,0:T(8,128)(2,1)S(1)}, bf16[2,256,256]{2,1,0:T(8,128)(2,1)}, u32[]{:S(2)}) copy-start(bf16[2,256,256]{2,1,0:T(8,128)(2,1)} %constant.14.clone.lanes_ref) | copy-start | bytes 786436

commit v2 on v1

--- a/solution.py
+++ b/solution.py
@@ -273,111 +273,140 @@
         out_ref[p, 1] = z[p][1]
 
 
-def forward_kernel(sec_ref, pre_ref, fwd_ref, x_ref, xp_ref, a_ref):
-    s = lax.axis_index("section")
-    x_first(pre_ref, a_ref)
-    for h in range(2):
-        u = 2 * s + h
-        xp_ref[pl.ds(h * 16, 16)] = x_unit(fwd_ref.at[u], a_ref[u])
-    x_first(sec_ref, a_ref)
-
-    @pl.loop(0, UNITS)
-    def _(u):
-        x_ref[pl.ds(u * 16, 16)] = x_unit(fwd_ref.at[u], a_ref[u])
-
-
-def middle_kernel(r_ref, rp_ref, lanes_ref, lanes_inv_ref, twist_ref, y_ref, v_ref, spec_ref, mirror_ref):
-    special = (lax.axis_index("section") == 0) & (lax.axis_index("row") == 0)
-    y_forward(rp_ref, twist_ref, lanes_ref, v_ref, spec_ref.at[1], mirror_ref.at[1], special)
-
-    @pl.loop(0, SEC)
-    def _(s):
-        own, prior = lax.rem(s, 2), lax.rem(s + 1, 2)
-        y_forward(r_ref.at[s], twist_ref, lanes_ref, v_ref, spec_ref.at[own], mirror_ref.at[own], special)
-        y_ratio(spec_ref.at[prior], spec_ref.at[own], mirror_ref.at[prior], mirror_ref.at[own], v_ref, special)
-        y_back(v_ref, twist_ref, lanes_inv_ref, y_ref.at[s])
-
-
-def back_kernel(q_ref, inv_ref, out_ref, top_ref, b_ref):
-    @pl.loop(0, UNITS)
-    def _(u):
-        value = q_ref[pl.ds(u * 16, 16)].reshape(2 * L, L)
-        b_ref[u] = table_times(inv_ref.at[u], value)
-
-    top_ref[...] = x_last(b_ref, out_ref)
-
-
 def here():
     return lax.axis_index("section"), lax.axis_index("row")
 
 
-def exchange_kernel(with_first, *refs):
-    if with_first:
-        x_ref, xp_ref, o_ref, op_ref, send_sem, recv_sem, loc_sem = refs
-    else:
-        x_ref, o_ref, send_sem, recv_sem, loc_sem = refs
+def kernel(
+    sec_hbm, pre_hbm, fwd_hbm, inv_hbm, lanes_hbm, lanes_inv_hbm, twist_hbm,
+    out_ref, peak_ref,
+    sec_ref, pre_ref, fwd_ref, inv_ref, lanes_ref, lanes_inv_ref, twist_ref,
+    a_ref, b_ref, x_ref, r_ref, y_ref, q_ref, v_ref, spec_ref, mirror_ref, mine_ref, all_ref,
+    load_sem, send_sem, there_sem, back_sem, top_sem,
+):
     s, p = here()
+    me = s * ROW + p
+    special = me == 0
+    loads = [
+        pltpu.make_async_copy(source, target, load_sem.at[i])
+        for i, (source, target) in enumerate(
+            (
+                (sec_hbm, sec_ref),
+                (fwd_hbm, fwd_ref),
+                (pre_hbm, pre_ref),
+                (twist_hbm, twist_ref),
+                (lanes_hbm, lanes_ref),
+                (lanes_inv_hbm, lanes_inv_ref),
+                (inv_hbm, inv_ref),
+            )
+        )
+    ]
+    for load in loads:
+        load.start()
+
     bar = pltpu.get_barrier_semaphore()
 
-    @pl.loop(1, DEV)
-    def _(i):
-        to = ((s + i // ROW) % SEC, (p + i % ROW) % ROW)
+    def greet(i, _):
+        to = ((s + (i >> 5)) & (SEC - 1), (p + i) & (ROW - 1))
         pl.semaphore_signal(bar, inc=1, device_id=to, device_id_type=MESH)
-
+        return 0
+
+    lax.fori_loop(1, DEV, greet, 0, unroll=5)
+
+    def send(group, source_ref, base, target_ref, mark, sem, ready, own):
+        if own:
+            pltpu.make_async_copy(source_ref.at[base + p], target_ref.at[mark], ready).start()
+
+        def one(i, _):
+            to = (p + i) & (ROW - 1)
+            pltpu.make_async_remote_copy(
+                source_ref.at[base + to], target_ref.at[mark], sem, ready, device_id=(group, to), device_id_type=MESH
+            ).start()
+            return 0
+
+        lax.fori_loop(1 if own else 0, ROW, one, 0)
+
+    def units(group, from_ref, base):
+        for h in range(2):
+            u = 2 * group + h
+            x_ref[pl.ds(base + h * 16, 16)] = x_unit(fwd_ref.at[u], from_ref[u])
+
+    loads[0].wait()
+    x_first(sec_ref, a_ref)
+    loads[1].wait()
+    units(s, a_ref, s * ROW)
     pl.semaphore_wait(bar, DEV - 1)
-    me = s * ROW + p
-    own = [pltpu.make_async_copy(x_ref.at[me], o_ref.at[me], loc_sem.at[0])]
-    if with_first:
-        own.append(pltpu.make_async_copy(xp_ref.at[p], op_ref.at[p], loc_sem.at[1]))
-    for copy in own:
-        copy.start()
-    if with_first:
-
-        @pl.loop(1, ROW)
-        def _(i):
-            to = (p + i) % ROW
-            pltpu.make_async_remote_copy(
-                xp_ref.at[to], op_ref.at[p], send_sem.at[1], recv_sem.at[1], device_id=(s, to), device_id_type=MESH
-            ).start()
-
-    @pl.loop(1, DEV)
-    def _(i):
-        ts, tp = (s + i // ROW) % SEC, (p + i % ROW) % ROW
+    send(s, x_ref, s * ROW, r_ref, me, send_sem.at[0], there_sem.at[0], True)
+    loads[2].wait()
+    x_first(pre_ref, b_ref)
+    units(s, b_ref, DEV)
+    send(s, x_ref, DEV, r_ref, DEV + p, send_sem.at[0], there_sem.at[1], True)
+
+    @pl.loop(1, SEC)
+    def _(t):
+        group = (s + t) & (SEC - 1)
+        units(group, a_ref, group * ROW)
+        send(group, x_ref, group * ROW, r_ref, me, send_sem.at[0], there_sem.at[t + 1], False)
+
+    for load in loads[3:6]:
+        load.wait()
+
+    @pl.loop(0, SEC + 2)
+    def _(k):
+        @pl.when(k < SEC + 1)
+        def _():
+            index = jnp.where(k == 1, SEC, (s - jnp.maximum(k - 1, 0)) & (SEC - 1))
+            tile = r_ref.at[pl.ds(index * ROW, ROW)]
+            pltpu.make_async_copy(tile, tile, there_sem.at[k]).wait()
+            y_forward(tile, twist_ref, lanes_ref, v_ref, spec_ref.at[index], mirror_ref.at[index], special)
+
+        @pl.when(k >= 2)
+        def _():
+            own = (s - k + 2) & (SEC - 1)
+            prior = jnp.where(own == 0, SEC, own - 1)
+            y_ratio(spec_ref.at[prior], spec_ref.at[own], mirror_ref.at[prior], mirror_ref.at[own], v_ref, special)
+            y_back(v_ref, twist_ref, lanes_inv_ref, y_ref.at[pl.ds(own * ROW, ROW)])
+
+            @pl.when(k == 2)
+            def _():
+                send(s, y_ref, s * ROW, q_ref, me, send_sem.at[1], back_sem.at[0], True)
+
+            @pl.when(k > 2)
+            def _():
+                send(own, y_ref, own * ROW, q_ref, me, send_sem.at[1], back_sem.at[k - 2], False)
+
+    loads[6].wait()
+
+    @pl.loop(0, SEC)
+    def _(m):
+        group = (s + m) & (SEC - 1)
+        tile = q_ref.at[pl.ds(group * ROW, ROW)]
+        pltpu.make_async_copy(tile, tile, back_sem.at[m]).wait()
+        for h in range(2):
+            u = 2 * group + h
+            b_ref[u] = table_times(inv_ref.at[u], q_ref[pl.ds(u * 16, 16)].reshape(2 * L, L))
+
+    top = x_last(b_ref, out_ref)
+
+    mine_ref[...] = top
+    all_ref[p] = top
+
+    def tell(i, _):
+        to = (p + i) & (ROW - 1)
         pltpu.make_async_remote_copy(
-            x_ref.at[ts * ROW + tp], o_ref.at[me], send_sem.at[0], recv_sem.at[0], device_id=(ts, tp), device_id_type=MESH
+            mine_ref, all_ref.at[p], top_sem.at[0], top_sem.at[1], device_id=(s, to), device_id_type=MESH
         ).start()
-
-    for copy in own:
-        copy.wait()
-    for sem in (recv_sem, send_sem):
-        count = pl.ds(0, DEV - 1)
-        pltpu.make_async_copy(x_ref.at[count], o_ref.at[count], sem.at[0]).wait()
-        if with_first:
-            count = pl.ds(0, ROW - 1)
-            pltpu.make_async_copy(xp_ref.at[count], op_ref.at[count], sem.at[1]).wait()
-
-
-def peak_kernel(top_ref, peak_ref, mine_ref, all_ref, send_sem, recv_sem):
-    s, p = here()
-    bar = pltpu.get_barrier_semaphore()
-
-    @pl.loop(1, ROW)
-    def _(i):
-        pl.semaphore_signal(bar, inc=1, device_id=(s, (p + i) % ROW), device_id_type=MESH)
-
-    pl.semaphore_wait(bar, ROW - 1)
-    mine_ref[...] = top_ref[...]
-    all_ref[p] = top_ref[...]
-
-    @pl.loop(1, ROW)
-    def _(i):
-        pltpu.make_async_remote_copy(
-            mine_ref, all_ref.at[p], send_sem, recv_sem, device_id=(s, (p + i) % ROW), device_id_type=MESH
-        ).start()
-
-    count = pl.ds(0, ROW - 1)
-    for sem in (recv_sem, send_sem):
-        pltpu.make_async_copy(all_ref.at[count], all_ref.at[count], sem).wait()
+        return 0
+
+    lax.fori_loop(1, ROW, tell, 0)
+
+    sent = r_ref.at[pl.ds(0, DEV + ROW - 2)]
+    pltpu.make_async_copy(sent, sent, send_sem.at[0]).wait()
+    sent = q_ref.at[pl.ds(0, DEV - 1)]
+    pltpu.make_async_copy(sent, sent, send_sem.at[1]).wait()
+    for i in range(2):
+        told = all_ref.at[pl.ds(0, ROW - 1)]
+        pltpu.make_async_copy(told, told, top_sem.at[i]).wait()
     peak_ref[...] = jnp.max(all_ref[...], axis=0)
 
 
@@ -389,44 +418,25 @@
     return jax.ShapeDtypeStruct(shape, F32)
 
 
-def call(kernel, args, outs, scratch, place=VMEM, collective=None):
-    extra = {} if collective is None else dict(collective_id=collective, has_side_effects=True)
-    return pl.pallas_call(
-        kernel,
-        out_shape=outs,
-        in_specs=[place] * len(args),
-        out_specs=jax.tree.map(lambda _: place, outs),
-        scratch_shapes=scratch,
-        compiler_params=pltpu.CompilerParams(vmem_limit_bytes=VMEM_LIMIT, **extra),
-    )(*args)
-
-
 def local(sections, preceding):
     fwd, inv, lanes, lanes_inv, twist = (jnp.asarray(t) for t in tables())
-    block = (2, 8, L)
+    args = (sections.reshape(R, L, L), preceding.reshape(R, L, L), fwd, inv, lanes, lanes_inv, twist)
     sem = pltpu.SemaphoreType.DMA
-    x, xp = call(
-        forward_kernel,
-        (sections.reshape(R, L, L), preceding.reshape(R, L, L), fwd),
-        (f32(DEV, *block), f32(ROW, *block)),
-        [pltpu.VMEM((UNITS, 2 * L, L), F32)],
-    )
-    r, rp = call(
-        functools.partial(exchange_kernel, True), (x, xp), (f32(DEV, *block), f32(ROW, *block)), [sem((2,))] * 3, ANY, 1
-    )
-    y = call(
-        middle_kernel,
-        (r.reshape(SEC, ROW, *block), rp, lanes, lanes_inv, twist),
-        f32(SEC, ROW, *block),
-        [pltpu.VMEM((R, 8, 2 * L), F32)] + [pltpu.VMEM((2, R, 8, 2 * L), F32)] * 2,
-    )
-    q = call(functools.partial(exchange_kernel, False), (y.reshape(DEV, *block),), f32(DEV, *block), [sem((2,))] * 3, ANY, 2)
-    surface, top = call(
-        back_kernel, (q, inv), (f32(R, L, L), f32(8, L)), [pltpu.VMEM((UNITS, 2 * L, L), F32)]
-    )
-    peak = call(
-        peak_kernel, (top,), f32(8, L), [pltpu.VMEM((8, L), F32), pltpu.VMEM((ROW, 8, L), F32), sem, sem], VMEM, 3
-    )
+    blocks = lambda count: pltpu.VMEM((count, 2, 8, L), F32)
+    surface, peak = pl.pallas_call(
+        kernel,
+        out_shape=(f32(R, L, L), f32(8, L)),
+        in_specs=[ANY] * len(args),
+        out_specs=(VMEM, VMEM),
+        scratch_shapes=[pltpu.VMEM(v.shape, v.dtype) for v in args]
+        + [pltpu.VMEM((UNITS, 2 * L, L), F32)] * 2
+        + [blocks(DEV + ROW), blocks(DEV + ROW), blocks(DEV), blocks(DEV)]
+        + [pltpu.VMEM((R, 8, 2 * L), F32)]
+        + [pltpu.VMEM((SEC + 1, R, 8, 2 * L), F32)] * 2
+        + [pltpu.VMEM((8, L), F32), pltpu.VMEM((ROW, 8, L), F32)]
+        + [sem((7,)), sem((2,)), sem((SEC + 1,)), sem((SEC,)), sem((2,))],
+        compiler_params=pltpu.CompilerParams(vmem_limit_bytes=VMEM_LIMIT, collective_id=1, has_side_effects=True),
+    )(*args)
     return surface.reshape(1, N, L), jnp.max(peak).reshape(1)
 
 

time: 172 us -> 132 us (0.77)
  Pallas kernels: 169 us -> 124 us
  local copies, waits for them, and re-layouts: 1.6 us -> 5.75 us
    pallas_call x6 -> x1, Pallas kernels: 169 us -> 124 us  [local(): pl.pallas_call(kernel, out_shape=(f32(R, L, L), f32(8, L)), in_specs=[ANY...]
    unnamed x8 -> x9, local copies, waits for them, and re-layouts: 1.6 us -> 5.75 us
where the time goes in v2:
time: 132 us; the launch traced here: 131 us
  Pallas kernels  124 us (94%)
  local copies, waits for them, and re-layouts  5.75 us (4%)
    pallas_call x1, Pallas kernels, local(): pl.pallas_call(kernel, out_shape=(f32(R, L, L), f32(8, L)), in_specs=[ANY...  124 us
    unnamed x9, local copies, waits for them, and re-layouts  5.75 us

profile of v2, /device:TPU:1, one launch (start us, length us, event | category | flops | bytes accessed | tf_op | source)
XLA Modules:
  0.0 131.4 jit_solution(17857231022294475131)
XLA Ops:
  0.6 0.0 copy-start
  0.6 1.6 %copy-done = f32[1,4096,128]{2,1,0:T(8,128)S(1)} copy-done((f32[1,4096,128]{2,1,0:T(8,128)S(1)}, f32[1,4096,128]{2,1,0:T(8,128)}, u32[]{:S(2)}) %copy-start) | copy-done | bytes 2097176
  2.2 0.0 copy-start.1
  2.2 1.0 copy-done.1
  3.2 0.0 copy-start.2
  3.2 0.9 copy-done.2
  4.1 0.0 copy-start.3
  4.1 0.9 copy-done.3
  5.1 124.4 %shard_map.86 = (f32[32,128,128]{2,1,0:T(8,128)S(1)}, f32[8,128]{1,0:T(8,128)S(1)}) custom-call(f32[32,128,128]{2,1,0:T(8,128)S(1)} %bitcast.5, f32[32,128,128]{2,1,0:T(8,128)} %bitcast.6, bf16[16,2,256,256]{3,2,1,0:T(8,128)(2,1)} %constant.12.clone.fwd_hbm, bf16[16,2,256,256]{3,2,1,0:T(8,128)(2,1)} %constant.13.clone.inv_hbm, ...), custom_call_target="tpu_custom_call" | custom-call | tf_op jit(solution)/shard_map/pallas_call | solution.py:426
  129.5 0.6 reduce_max.9
  130.1 1.3 %copy.10 = f32[1,4096,128]{2,1,0:T(8,128)} copy(f32[1,4096,128]{2,1,0:T(8,128)S(1)} %bitcast.4) | data formatting | bytes 4194304
Async XLA Ops:
  0.6 1.6 %copy-start = (f32[1,4096,128]{2,1,0:T(8,128)S(1)}, f32[1,4096,128]{2,1,0:T(8,128)}, u32[]{:S(2)}) copy-start(f32[1,4096,128]{2,1,0:T(8,128)} %param.7) | copy-start | bytes 6291460
  2.2 1.0 copy-start.1
  3.2 0.9 copy-start.2
  4.1 0.9 copy-start.3

commit v3 on v2

--- a/solution.py
+++ b/solution.py
@@ -20,6 +20,7 @@
 SEC = 8
 ROW = 32
 DEV = SEC * ROW
+PADDED = 512
 UNITS = 16
 FLOOR = 0.02 * 4096 * 4096
 VMEM_LIMIT = 48 << 20
@@ -61,16 +62,15 @@
         fwd[0, js, 0, :, half], fwd[0, js, 1, :, half] = tr, ti
         inv[0, half, :, js, 0] = np.moveaxis(br, 2, 0)
         inv[0, half, :, js, 1] = np.moveaxis(bi, 2, 0)
-    fwd = split(fwd.reshape(UNITS, 2 * L, 2 * L))
-    inv = split(inv.reshape(UNITS, 2 * L, 2 * L) / N)
+    fwd, inv = fwd.reshape(UNITS, 2 * L, 2 * L), inv.reshape(UNITS, 2 * L, 2 * L) / N
     turn = 2 * np.pi / L * (np.outer(row, row) % L)
     c, s = np.cos(turn), np.sin(turn)
-    lanes = split(np.block([[c, -s], [s, c]]))
-    lanes_inv = split(np.block([[c, s], [-s, c]]))
+    fwd = split(np.concatenate([fwd, np.block([[c, -s], [s, c]])[None]]))
+    inv = split(np.concatenate([inv, np.block([[c, s], [-s, c]])[None]]))
     turn = 2 * np.pi / N * np.outer(np.arange(R + 1), row)
     twist = np.stack([np.cos(turn), np.sin(turn)], 1).astype(np.float32)
     twist = np.broadcast_to(twist[:, :, None, :], (R + 1, 2, 8, L)).copy()
-    return fwd, inv, lanes, lanes_inv, twist
+    return fwd, inv, np.pad(twist, ((0, PADDED - R - 1), (0, 0), (0, 0), (0, 0)))
 
 
 def turned(z, k, n, sign):
@@ -277,12 +277,19 @@
     return lax.axis_index("section"), lax.axis_index("row")
 
 
+def partner(p, j):
+    zj, yj, cj = j >> 3, (j >> 1) & 3, j & 1
+    dz, dy = zj ^ (zj >> 1) ^ 2, yj ^ (yj >> 1) ^ 2
+    z, y, core = ((p >> 3) + dz) & 3, ((p >> 1) + dy) & 3, (p & 1) ^ (1 - cj)
+    return z * 8 + y * 2 + core
+
+
 def kernel(
-    sec_hbm, pre_hbm, fwd_hbm, inv_hbm, lanes_hbm, lanes_inv_hbm, twist_hbm,
+    sec_hbm, pre_hbm, fwd_hbm, inv_hbm, twist_hbm,
     out_ref, peak_ref,
-    sec_ref, pre_ref, fwd_ref, inv_ref, lanes_ref, lanes_inv_ref, twist_ref,
+    sec_ref, pre_ref, fwd_ref, inv_ref, twist_ref,
     a_ref, b_ref, x_ref, r_ref, y_ref, q_ref, v_ref, spec_ref, mirror_ref, mine_ref, all_ref,
-    load_sem, send_sem, there_sem, back_sem, top_sem,
+    load_sem, send_sem, there_sem, back_sem, top_sem, go_sem,
 ):
     s, p = here()
     me = s * ROW + p
@@ -294,37 +301,34 @@
                 (sec_hbm, sec_ref),
                 (fwd_hbm, fwd_ref),
                 (pre_hbm, pre_ref),
-                (twist_hbm, twist_ref),
-                (lanes_hbm, lanes_ref),
-                (lanes_inv_hbm, lanes_inv_ref),
+                (twist_hbm.at[pl.ds(0, R + 1)], twist_ref),
                 (inv_hbm, inv_ref),
             )
         )
     ]
-    for load in loads:
-        load.start()
+    loads[0].start()
+    loads[1].start()
 
     bar = pltpu.get_barrier_semaphore()
 
-    def greet(i, _):
-        to = ((s + (i >> 5)) & (SEC - 1), (p + i) & (ROW - 1))
-        pl.semaphore_signal(bar, inc=1, device_id=to, device_id_type=MESH)
+    def greet(j, _):
+        pl.semaphore_signal(bar, inc=1, device_id=(s, partner(p, j)), device_id_type=MESH)
         return 0
 
-    lax.fori_loop(1, DEV, greet, 0, unroll=5)
+    lax.fori_loop(0, ROW - 1, greet, 0)
 
     def send(group, source_ref, base, target_ref, mark, sem, ready, own):
         if own:
             pltpu.make_async_copy(source_ref.at[base + p], target_ref.at[mark], ready).start()
 
-        def one(i, _):
-            to = (p + i) & (ROW - 1)
+        def one(j, _):
+            to = partner(p, j)
             pltpu.make_async_remote_copy(
                 source_ref.at[base + to], target_ref.at[mark], sem, ready, device_id=(group, to), device_id_type=MESH
             ).start()
             return 0
 
-        lax.fori_loop(1 if own else 0, ROW, one, 0)
+        lax.fori_loop(0, ROW - 1 if own else ROW, one, 0)
 
     def units(group, from_ref, base):
         for h in range(2):
@@ -332,24 +336,50 @@
             x_ref[pl.ds(base + h * 16, 16)] = x_unit(fwd_ref.at[u], from_ref[u])
 
     loads[0].wait()
+    for load in loads[2:]:
+        load.start()
     x_first(sec_ref, a_ref)
     loads[1].wait()
     units(s, a_ref, s * ROW)
-    pl.semaphore_wait(bar, DEV - 1)
+
+    @pl.when(p != 1)
+    def _():
+        pl.semaphore_wait(bar, ROW - 1)
+
+    @pl.when(p == 0)
+    def _():
+        for t in range(1, SEC):
+            pl.semaphore_signal(bar, inc=1, device_id=((s + t) & (SEC - 1), 1), device_id_type=MESH)
+
+    @pl.when(p == 1)
+    def _():
+        pl.semaphore_wait(bar, ROW - 1 + SEC - 1)
+
+        def release(j, _):
+            pl.semaphore_signal(go_sem, inc=1, device_id=(s, partner(p, j)), device_id_type=MESH)
+            return 0
+
+        lax.fori_loop(0, ROW - 1, release, 0)
+
     send(s, x_ref, s * ROW, r_ref, me, send_sem.at[0], there_sem.at[0], True)
     loads[2].wait()
     x_first(pre_ref, b_ref)
     units(s, b_ref, DEV)
     send(s, x_ref, DEV, r_ref, DEV + p, send_sem.at[0], there_sem.at[1], True)
 
+    @pl.when(p != 1)
+    def _():
+        pl.semaphore_wait(go_sem, 1)
+
     @pl.loop(1, SEC)
     def _(t):
         group = (s + t) & (SEC - 1)
         units(group, a_ref, group * ROW)
         send(group, x_ref, group * ROW, r_ref, me, send_sem.at[0], there_sem.at[t + 1], False)
 
-    for load in loads[3:6]:
+    for load in loads[3:]:
         load.wait()
+    lanes_ref, lanes_inv_ref = fwd_ref.at[UNITS], inv_ref.at[UNITS]
 
     @pl.loop(0, SEC + 2)
     def _(k):
@@ -375,8 +405,6 @@
             def _():
                 send(own, y_ref, own * ROW, q_ref, me, send_sem.at[1], back_sem.at[k - 2], False)
 
-    loads[6].wait()
-
     @pl.loop(0, SEC)
     def _(m):
         group = (s + m) & (SEC - 1)
@@ -391,14 +419,14 @@
     mine_ref[...] = top
     all_ref[p] = top
 
-    def tell(i, _):
-        to = (p + i) & (ROW - 1)
+    def tell(j, _):
+        to = partner(p, j)
         pltpu.make_async_remote_copy(
             mine_ref, all_ref.at[p], top_sem.at[0], top_sem.at[1], device_id=(s, to), device_id_type=MESH
         ).start()
         return 0
 
-    lax.fori_loop(1, ROW, tell, 0)
+    lax.fori_loop(0, ROW - 1, tell, 0)
 
     sent = r_ref.at[pl.ds(0, DEV + ROW - 2)]
     pltpu.make_async_copy(sent, sent, send_sem.at[0]).wait()
@@ -407,11 +435,12 @@
     for i in range(2):
         told = all_ref.at[pl.ds(0, ROW - 1)]
         pltpu.make_async_copy(told, told, top_sem.at[i]).wait()
-    peak_ref[...] = jnp.max(all_ref[...], axis=0)
+    peak_ref[0] = jnp.max(all_ref[...])
 
 
 VMEM = pl.BlockSpec(memory_space=pltpu.VMEM)
-ANY = pl.BlockSpec(memory_space=pl.ANY)
+SMEM = pl.BlockSpec(memory_space=pltpu.SMEM)
+HBM = pl.BlockSpec(memory_space=pltpu.HBM)
 
 
 def f32(*shape):
@@ -419,25 +448,26 @@
 
 
 def local(sections, preceding):
-    fwd, inv, lanes, lanes_inv, twist = (jnp.asarray(t) for t in tables())
-    args = (sections.reshape(R, L, L), preceding.reshape(R, L, L), fwd, inv, lanes, lanes_inv, twist)
+    fwd, inv, twist = (jnp.asarray(t) for t in tables())
+    args = (sections.reshape(R, L, L), preceding.reshape(R, L, L), fwd, inv, twist)
     sem = pltpu.SemaphoreType.DMA
     blocks = lambda count: pltpu.VMEM((count, 2, 8, L), F32)
     surface, peak = pl.pallas_call(
         kernel,
-        out_shape=(f32(R, L, L), f32(8, L)),
-        in_specs=[ANY] * len(args),
-        out_specs=(VMEM, VMEM),
-        scratch_shapes=[pltpu.VMEM(v.shape, v.dtype) for v in args]
+        out_shape=(f32(R, L, L), f32(1)),
+        in_specs=[HBM] * len(args),
+        out_specs=(VMEM, SMEM),
+        scratch_shapes=[pltpu.VMEM(v.shape, v.dtype) for v in args[:4]]
+        + [pltpu.VMEM((R + 1, 2, 8, L), F32)]
         + [pltpu.VMEM((UNITS, 2 * L, L), F32)] * 2
         + [blocks(DEV + ROW), blocks(DEV + ROW), blocks(DEV), blocks(DEV)]
         + [pltpu.VMEM((R, 8, 2 * L), F32)]
         + [pltpu.VMEM((SEC + 1, R, 8, 2 * L), F32)] * 2
         + [pltpu.VMEM((8, L), F32), pltpu.VMEM((ROW, 8, L), F32)]
-        + [sem((7,)), sem((2,)), sem((SEC + 1,)), sem((SEC,)), sem((2,))],
+        + [sem((5,)), sem((2,)), sem((SEC + 1,)), sem((SEC,)), sem((2,)), pltpu.SemaphoreType.REGULAR],
         compiler_params=pltpu.CompilerParams(vmem_limit_bytes=VMEM_LIMIT, collective_id=1, has_side_effects=True),
     )(*args)
-    return surface.reshape(1, N, L), jnp.max(peak).reshape(1)
+    return surface.reshape(1, N, L), peak
 
 
 def solution(mesh):

time: 132 us -> 127 us (0.962)
  Pallas kernels: 124 us -> 121 us
  local copies, waits for them, and re-layouts: 5.75 us -> 2.91 us
  between operations: 0.65 us -> 2.41 us
    pallas_call x1, Pallas kernels: 124 us -> 121 us  [local(): pl.pallas_call(kernel, out_shape=(f32(R, L, L), f32(1)), in_specs=[HBM] *...]
    unnamed x9 -> x3, local copies, waits for them, and re-layouts: 5.75 us -> 2.91 us
where the time goes in v3:
time: 127 us; the launch traced here: 126 us
  Pallas kernels  121 us (95%)
  local copies, waits for them, and re-layouts  2.91 us (2%)
  between operations  2.41 us (2%)
    pallas_call x1, Pallas kernels, local(): pl.pallas_call(kernel, out_shape=(f32(R, L, L), f32(1)), in_specs=[HBM] *...  121 us
    unnamed x3, local copies, waits for them, and re-layouts  2.91 us

profile of v3, /device:TPU:1, one launch (start us, length us, event | category | flops | bytes accessed | tf_op | source)
XLA Modules:
  0.0 126.5 jit_solution(11035297627152976181)
XLA Ops:
  0.6 0.0 copy-start
  0.6 1.6 %copy-done = f32[1,4096,128]{2,1,0:T(8,128)S(1)} copy-done((f32[1,4096,128]{2,1,0:T(8,128)S(1)}, f32[1,4096,128]{2,1,0:T(8,128)}, u32[]{:S(2)}) %copy-start) | copy-done | bytes 2097176
  2.2 121.2 %shard_map.68 = (f32[32,128,128]{2,1,0:T(8,128)S(1)}, f32[1]{0:T(128)}) custom-call(f32[32,128,128]{2,1,0:T(8,128)S(1)} %bitcast.3, f32[32,128,128]{2,1,0:T(8,128)} %bitcast.5, bf16[17,2,256,256]{3,2,1,0:T(8,128)(2,1)} %constant.6.clone.fwd_hbm, bf16[17,2,256,256]{3,2,1,0:T(8,128)(2,1)} %constant.7.clone.inv_hbm, f32[512,2,8,128]{3,2,1,0:T(8,128)} %constant.8.clone.twist_hbm), custom_call_target="tpu_custom_call" | custom-call | tf_op jit(solution)/shard_map/pallas_call | solution.py:455
  123.4 1.3 %copy.9 = f32[1,4096,128]{2,1,0:T(8,128)} copy(f32[1,4096,128]{2,1,0:T(8,128)S(1)} %bitcast.4) | data formatting | bytes 4194304
Async XLA Ops:
  0.6 1.6 %copy-start = (f32[1,4096,128]{2,1,0:T(8,128)S(1)}, f32[1,4096,128]{2,1,0:T(8,128)}, u32[]{:S(2)}) copy-start(f32[1,4096,128]{2,1,0:T(8,128)} %param.5) | copy-start | bytes 6291460

commit v4 on v3

--- a/solution.py
+++ b/solution.py
@@ -23,7 +23,7 @@
 PADDED = 512
 UNITS = 16
 FLOOR = 0.02 * 4096 * 4096
-VMEM_LIMIT = 48 << 20
+VMEM_LIMIT = 50 << 20
 
 
 def split(table):
@@ -288,7 +288,7 @@
     sec_hbm, pre_hbm, fwd_hbm, inv_hbm, twist_hbm,
     out_ref, peak_ref,
     sec_ref, pre_ref, fwd_ref, inv_ref, twist_ref,
-    a_ref, b_ref, x_ref, r_ref, y_ref, q_ref, v_ref, spec_ref, mirror_ref, mine_ref, all_ref,
+    near_ref, a_ref, b_ref, x_ref, r_ref, y_ref, q_ref, v_ref, spec_ref, mirror_ref, mine_ref, all_ref,
     load_sem, send_sem, there_sem, back_sem, top_sem, go_sem,
 ):
     s, p = here()
@@ -299,8 +299,9 @@
         for i, (source, target) in enumerate(
             (
                 (sec_hbm, sec_ref),
+                (fwd_hbm.at[pl.ds(2 * s, 2)], near_ref),
+                (pre_hbm, pre_ref),
                 (fwd_hbm, fwd_ref),
-                (pre_hbm, pre_ref),
                 (twist_hbm.at[pl.ds(0, R + 1)], twist_ref),
                 (inv_hbm, inv_ref),
             )
@@ -330,46 +331,43 @@
 
         lax.fori_loop(0, ROW - 1 if own else ROW, one, 0)
 
-    def units(group, from_ref, base):
+    def units(group, from_ref, base, table_ref=None):
         for h in range(2):
             u = 2 * group + h
-            x_ref[pl.ds(base + h * 16, 16)] = x_unit(fwd_ref.at[u], from_ref[u])
+            table = fwd_ref.at[u] if table_ref is None else table_ref.at[h]
+            x_ref[pl.ds(base + h * 16, 16)] = x_unit(table, from_ref[u])
 
     loads[0].wait()
     for load in loads[2:]:
         load.start()
     x_first(sec_ref, a_ref)
     loads[1].wait()
-    units(s, a_ref, s * ROW)
-
-    @pl.when(p != 1)
+    units(s, a_ref, s * ROW, near_ref)
+
+    second = (p & 1) == 1
+
+    @pl.when(jnp.logical_not(second))
     def _():
         pl.semaphore_wait(bar, ROW - 1)
-
-    @pl.when(p == 0)
-    def _():
         for t in range(1, SEC):
-            pl.semaphore_signal(bar, inc=1, device_id=((s + t) & (SEC - 1), 1), device_id_type=MESH)
-
-    @pl.when(p == 1)
+            pl.semaphore_signal(bar, inc=1, device_id=((s + t) & (SEC - 1), p + 1), device_id_type=MESH)
+
+    @pl.when(second)
     def _():
         pl.semaphore_wait(bar, ROW - 1 + SEC - 1)
-
-        def release(j, _):
-            pl.semaphore_signal(go_sem, inc=1, device_id=(s, partner(p, j)), device_id_type=MESH)
-            return 0
-
-        lax.fori_loop(0, ROW - 1, release, 0)
+        pl.semaphore_signal(go_sem, inc=1, device_id=(s, p - 1), device_id_type=MESH)
 
     send(s, x_ref, s * ROW, r_ref, me, send_sem.at[0], there_sem.at[0], True)
     loads[2].wait()
     x_first(pre_ref, b_ref)
-    units(s, b_ref, DEV)
+    units(s, b_ref, DEV, near_ref)
     send(s, x_ref, DEV, r_ref, DEV + p, send_sem.at[0], there_sem.at[1], True)
 
-    @pl.when(p != 1)
+    @pl.when(jnp.logical_not(second))
     def _():
         pl.semaphore_wait(go_sem, 1)
+
+    loads[3].wait()
 
     @pl.loop(1, SEC)
     def _(t):
@@ -377,7 +375,7 @@
         units(group, a_ref, group * ROW)
         send(group, x_ref, group * ROW, r_ref, me, send_sem.at[0], there_sem.at[t + 1], False)
 
-    for load in loads[3:]:
+    for load in loads[4:]:
         load.wait()
     lanes_ref, lanes_inv_ref = fwd_ref.at[UNITS], inv_ref.at[UNITS]
 
@@ -458,13 +456,13 @@
         in_specs=[HBM] * len(args),
         out_specs=(VMEM, SMEM),
         scratch_shapes=[pltpu.VMEM(v.shape, v.dtype) for v in args[:4]]
-        + [pltpu.VMEM((R + 1, 2, 8, L), F32)]
+        + [pltpu.VMEM((R + 1, 2, 8, L), F32), pltpu.VMEM((2, 2, 2 * L, 2 * L), BF16)]
         + [pltpu.VMEM((UNITS, 2 * L, L), F32)] * 2
         + [blocks(DEV + ROW), blocks(DEV + ROW), blocks(DEV), blocks(DEV)]
         + [pltpu.VMEM((R, 8, 2 * L), F32)]
         + [pltpu.VMEM((SEC + 1, R, 8, 2 * L), F32)] * 2
         + [pltpu.VMEM((8, L), F32), pltpu.VMEM((ROW, 8, L), F32)]
-        + [sem((5,)), sem((2,)), sem((SEC + 1,)), sem((SEC,)), sem((2,)), pltpu.SemaphoreType.REGULAR],
+        + [sem((6,)), sem((2,)), sem((SEC + 1,)), sem((SEC,)), sem((2,)), pltpu.SemaphoreType.REGULAR],
         compiler_params=pltpu.CompilerParams(vmem_limit_bytes=VMEM_LIMIT, collective_id=1, has_side_effects=True),
     )(*args)
     return surface.reshape(1, N, L), peak

time: 127 us -> 125 us (0.984)
  local copies, waits for them, and re-layouts: 2.91 us -> 1.32 us
    unnamed x3 -> x1, local copies, waits for them, and re-layouts: 2.91 us -> 1.32 us
where the time goes in v4:
time: 125 us
  Pallas kernels  121 us (97%)
  between operations  2.33 us (2%)
  local copies, waits for them, and re-layouts  1.32 us (1%)
    pallas_call x1, Pallas kernels, local(): pl.pallas_call(kernel, out_shape=(f32(R, L, L), f32(1)), in_specs=[HBM] *...  121 us

profile of v4, /device:TPU:1, one launch (start us, length us, event | category | flops | bytes accessed | tf_op | source)
XLA Modules:
  0.0 124.9 jit_solution(11184724348177294770)
XLA Ops:
  0.6 121.2 %shard_map.68 = (f32[32,128,128]{2,1,0:T(8,128)S(1)}, f32[1]{0:T(128)}) custom-call(f32[32,128,128]{2,1,0:T(8,128)} %bitcast.4, f32[32,128,128]{2,1,0:T(8,128)} %bitcast.5, bf16[17,2,256,256]{3,2,1,0:T(8,128)(2,1)} %constant.6.clone.fwd_hbm, bf16[17,2,256,256]{3,2,1,0:T(8,128)(2,1)} %constant.7.clone.inv_hbm, f32[512,2,8,128]{3,2,1,0:T(8,128)} %constant.8.clone.twist_hbm), custom_call_target="tpu_custom_call" | custom-call | tf_op jit(solution)/shard_map/pallas_call | solution.py:453
  121.9 1.3 %copy.9 = f32[1,4096,128]{2,1,0:T(8,128)} copy(f32[1,4096,128]{2,1,0:T(8,128)S(1)} %bitcast.3) | data formatting | bytes 4194304

commit v5 on v4

--- a/solution.py
+++ b/solution.py
@@ -21,6 +21,7 @@
 ROW = 32
 DEV = SEC * ROW
 PADDED = 512
+AHEAD = 3
 UNITS = 16
 FLOOR = 0.02 * 4096 * 4096
 VMEM_LIMIT = 50 << 20
@@ -277,11 +278,33 @@
     return lax.axis_index("section"), lax.axis_index("row")
 
 
-def partner(p, j):
-    zj, yj, cj = j >> 3, (j >> 1) & 3, j & 1
-    dz, dy = zj ^ (zj >> 1) ^ 2, yj ^ (yj >> 1) ^ 2
-    z, y, core = ((p >> 3) + dz) & 3, ((p >> 1) + dy) & 3, (p & 1) ^ (1 - cj)
-    return z * 8 + y * 2 + core
+def partners(p, step, count):
+    dz = step ^ (step >> 1) ^ 2
+    z = (((p >> 3) + dz) & 3) * 8
+    for dy in (2, 3, 1, 0):
+        y = (((p >> 1) + dy) & 3) * 2 + z
+        for flip in (1, 0):
+            if count:
+                count -= 1
+                yield y + ((p & 1) ^ flip)
+
+
+def each_partner(p, act, own):
+    if own:
+
+        @pl.loop(0, 3)
+        def _(step):
+            for to in partners(p, step, 8):
+                act(to)
+
+        for to in partners(p, 3, 7):
+            act(to)
+    else:
+
+        @pl.loop(0, 4)
+        def _(step):
+            for to in partners(p, step, 8):
+                act(to)
 
 
 def kernel(
@@ -312,24 +335,18 @@
 
     bar = pltpu.get_barrier_semaphore()
 
-    def greet(j, _):
-        pl.semaphore_signal(bar, inc=1, device_id=(s, partner(p, j)), device_id_type=MESH)
-        return 0
-
-    lax.fori_loop(0, ROW - 1, greet, 0)
+    each_partner(p, lambda to: pl.semaphore_signal(bar, inc=1, device_id=(s, to), device_id_type=MESH), True)
 
     def send(group, source_ref, base, target_ref, mark, sem, ready, own):
         if own:
             pltpu.make_async_copy(source_ref.at[base + p], target_ref.at[mark], ready).start()
 
-        def one(j, _):
-            to = partner(p, j)
+        def one(to):
             pltpu.make_async_remote_copy(
                 source_ref.at[base + to], target_ref.at[mark], sem, ready, device_id=(group, to), device_id_type=MESH
             ).start()
-            return 0
-
-        lax.fori_loop(0, ROW - 1 if own else ROW, one, 0)
+
+        each_partner(p, one, own)
 
     def units(group, from_ref, base, table_ref=None):
         for h in range(2):
@@ -369,11 +386,12 @@
 
     loads[3].wait()
 
-    @pl.loop(1, SEC)
-    def _(t):
+    def slot(t):
         group = (s + t) & (SEC - 1)
         units(group, a_ref, group * ROW)
         send(group, x_ref, group * ROW, r_ref, me, send_sem.at[0], there_sem.at[t + 1], False)
+
+    pl.loop(1, AHEAD)(slot)
 
     for load in loads[4:]:
         load.wait()
@@ -386,6 +404,11 @@
             index = jnp.where(k == 1, SEC, (s - jnp.maximum(k - 1, 0)) & (SEC - 1))
             tile = r_ref.at[pl.ds(index * ROW, ROW)]
             pltpu.make_async_copy(tile, tile, there_sem.at[k]).wait()
+
+            @pl.when(k < SEC - AHEAD)
+            def _():
+                slot(k + AHEAD)
+
             y_forward(tile, twist_ref, lanes_ref, v_ref, spec_ref.at[index], mirror_ref.at[index], special)
 
         @pl.when(k >= 2)
@@ -417,14 +440,12 @@
     mine_ref[...] = top
     all_ref[p] = top
 
-    def tell(j, _):
-        to = partner(p, j)
+    def tell(to):
         pltpu.make_async_remote_copy(
             mine_ref, all_ref.at[p], top_sem.at[0], top_sem.at[1], device_id=(s, to), device_id_type=MESH
         ).start()
-        return 0
-
-    lax.fori_loop(0, ROW - 1, tell, 0)
+
+    each_partner(p, tell, True)
 
     sent = r_ref.at[pl.ds(0, DEV + ROW - 2)]
     pltpu.make_async_copy(sent, sent, send_sem.at[0]).wait()

time: 125 us -> 124 us (level)
  no operation moved by 1% of the time
where the time goes in v5:
time: 124 us
  Pallas kernels  121 us (98%)
  between operations  2.33 us (2%)
  local copies, waits for them, and re-layouts  1.32 us (1%)
    pallas_call x1, Pallas kernels, local(): pl.pallas_call(kernel, out_shape=(f32(R, L, L), f32(1)), in_specs=[HBM] *...  121 us

profile of v5, /device:TPU:1, one launch (start us, length us, event | category | flops | bytes accessed | tf_op | source)
XLA Modules:
  0.0 124.3 jit_solution(11403729528908135021)
XLA Ops:
  0.6 120.7 %shard_map.68 = (f32[32,128,128]{2,1,0:T(8,128)S(1)}, f32[1]{0:T(128)}) custom-call(f32[32,128,128]{2,1,0:T(8,128)} %bitcast.4, f32[32,128,128]{2,1,0:T(8,128)} %bitcast.5, bf16[17,2,256,256]{3,2,1,0:T(8,128)(2,1)} %constant.6.clone.fwd_hbm, bf16[17,2,256,256]{3,2,1,0:T(8,128)(2,1)} %constant.7.clone.inv_hbm, f32[512,2,8,128]{3,2,1,0:T(8,128)} %constant.8.clone.twist_hbm), custom_call_target="tpu_custom_call" | custom-call | tf_op jit(solution)/shard_map/pallas_call | solution.py:474
  121.3 1.3 %copy.9 = f32[1,4096,128]{2,1,0:T(8,128)} copy(f32[1,4096,128]{2,1,0:T(8,128)S(1)} %bitcast.3) | data formatting | bytes 4194304

commit v6 on v5

--- a/solution.py
+++ b/solution.py
@@ -317,6 +317,10 @@
     s, p = here()
     me = s * ROW + p
     special = me == 0
+    bar = pltpu.get_barrier_semaphore()
+
+    each_partner(p, lambda to: pl.semaphore_signal(bar, inc=1, device_id=(s, to), device_id_type=MESH), True)
+
     loads = [
         pltpu.make_async_copy(source, target, load_sem.at[i])
         for i, (source, target) in enumerate(
@@ -333,10 +337,6 @@
     loads[0].start()
     loads[1].start()
 
-    bar = pltpu.get_barrier_semaphore()
-
-    each_partner(p, lambda to: pl.semaphore_signal(bar, inc=1, device_id=(s, to), device_id_type=MESH), True)
-
     def send(group, source_ref, base, target_ref, mark, sem, ready, own):
         if own:
             pltpu.make_async_copy(source_ref.at[base + p], target_ref.at[mark], ready).start()
@@ -437,6 +437,7 @@
 
     top = x_last(b_ref, out_ref)
 
+    top = jnp.max(top, axis=0, keepdims=True)
     mine_ref[...] = top
     all_ref[p] = top
 
@@ -482,7 +483,7 @@
         + [blocks(DEV + ROW), blocks(DEV + ROW), blocks(DEV), blocks(DEV)]
         + [pltpu.VMEM((R, 8, 2 * L), F32)]
         + [pltpu.VMEM((SEC + 1, R, 8, 2 * L), F32)] * 2
-        + [pltpu.VMEM((8, L), F32), pltpu.VMEM((ROW, 8, L), F32)]
+        + [pltpu.VMEM((1, L), F32), pltpu.VMEM((ROW, 1, L), F32)]
         + [sem((6,)), sem((2,)), sem((SEC + 1,)), sem((SEC,)), sem((2,)), pltpu.SemaphoreType.REGULAR],
         compiler_params=pltpu.CompilerParams(vmem_limit_bytes=VMEM_LIMIT, collective_id=1, has_side_effects=True),
     )(*args)

time: 124 us -> 124 us (level)
  no operation moved by 1% of the time
where the time goes in v6:
time: 124 us
  Pallas kernels  120 us (97%)
  between operations  2.33 us (2%)
  local copies, waits for them, and re-layouts  1.32 us (1%)
    pallas_call x1, Pallas kernels, local(): pl.pallas_call(kernel, out_shape=(f32(R, L, L), f32(1)), in_specs=[HBM] *...  120 us

profile of v6, /device:TPU:1, one launch (start us, length us, event | category | flops | bytes accessed | tf_op | source)
XLA Modules:
  0.0 123.7 jit_solution(15242665425301246739)
XLA Ops:
  0.6 120.0 %shard_map.68 = (f32[32,128,128]{2,1,0:T(8,128)S(1)}, f32[1]{0:T(128)}) custom-call(f32[32,128,128]{2,1,0:T(8,128)} %bitcast.4, f32[32,128,128]{2,1,0:T(8,128)} %bitcast.5, bf16[17,2,256,256]{3,2,1,0:T(8,128)(2,1)} %constant.6.clone.fwd_hbm, bf16[17,2,256,256]{3,2,1,0:T(8,128)(2,1)} %constant.7.clone.inv_hbm, f32[512,2,8,128]{3,2,1,0:T(8,128)} %constant.8.clone.twist_hbm), custom_call_target="tpu_custom_call" | custom-call | tf_op jit(solution)/shard_map/pallas_call | solution.py:475
  120.7 1.3 %copy.9 = f32[1,4096,128]{2,1,0:T(8,128)} copy(f32[1,4096,128]{2,1,0:T(8,128)S(1)} %bitcast.3) | data formatting | bytes 4194304

commit v7 on v6

--- a/solution.py
+++ b/solution.py
@@ -197,7 +197,7 @@
             out = [jnp.maximum(a, b) for a, b in zip(out[0::2], out[1::2])]
         return jnp.maximum(top, out[0])
 
-    return lax.fori_loop(0, L // 8, body, jnp.full((8, L), -jnp.inf, F32))
+    return lax.fori_loop(0, L // 8, body, jnp.full((8, L), -jnp.inf, F32), unroll=2)
 
 
 def y_forward(tile_ref, twist_ref, lanes_ref, v_ref, own_ref, mirror_ref, special):

time: 124 us -> 124 us (level)
  no operation moved by 1% of the time
where the time goes in v7:
time: 124 us
  Pallas kernels  120 us (97%)
  between operations  2.33 us (2%)
  local copies, waits for them, and re-layouts  1.32 us (1%)
    pallas_call x1, Pallas kernels, local(): pl.pallas_call(kernel, out_shape=(f32(R, L, L), f32(1)), in_specs=[HBM] *...  120 us

profile of v7, /device:TPU:1, one launch (start us, length us, event | category | flops | bytes accessed | tf_op | source)
XLA Modules:
  0.0 123.5 jit_solution(13099787288406270241)
XLA Ops:
  0.6 119.9 %shard_map.68 = (f32[32,128,128]{2,1,0:T(8,128)S(1)}, f32[1]{0:T(128)}) custom-call(f32[32,128,128]{2,1,0:T(8,128)} %bitcast.4, f32[32,128,128]{2,1,0:T(8,128)} %bitcast.5, bf16[17,2,256,256]{3,2,1,0:T(8,128)(2,1)} %constant.6.clone.fwd_hbm, bf16[17,2,256,256]{3,2,1,0:T(8,128)(2,1)} %constant.7.clone.inv_hbm, f32[512,2,8,128]{3,2,1,0:T(8,128)} %constant.8.clone.twist_hbm), custom_call_target="tpu_custom_call" | custom-call | tf_op jit(solution)/shard_map/pallas_call | solution.py:475
  120.5 1.3 %copy.9 = f32[1,4096,128]{2,1,0:T(8,128)} copy(f32[1,4096,128]{2,1,0:T(8,128)S(1)} %bitcast.3) | data formatting | bytes 4194304
